TPU v7x, 32 devices: a whole 2x2x4 slice. The times are simulated.
32 devices in a mesh: dp: 8 (over y, x, core), tensor: 4 (over z).
Axes of the slice: x: 2, y: 2, z: 4, core: 2. Of those that a mesh axis runs over, the one named last changes fastest.
Arguments:
- tokens: bfloat16 [8192, 8192], P('dp', 'tensor'), may hold values from -6 to 6
- packing: int32 [8, 6], replicated, may hold values from 0 to 63, as said below
- tail_tokens: int32 [8], replicated, may hold values from 1 to 128
- mix_ratio: int32 [2], replicated, may hold values from 1 to 32, as said below
- policy_gate: bfloat16 [8192, 14336], P(('dp', 'tensor')), may hold values from -6 to 6
- policy_up: bfloat16 [8192, 14336], P(('dp', 'tensor')), may hold values from -6 to 6
- reference_gate: bfloat16 [8192, 14336], P('dp', 'tensor'), may hold values from -6 to 6
- reference_up: bfloat16 [8192, 14336], P('dp', 'tensor'), may hold values from -6 to 6
Outputs:
- new_gate: bfloat16 [8192, 14336], P('dp', 'tensor')
- new_up: bfloat16 [8192, 14336], P('dp', 'tensor')
- hidden: bfloat16 [6144, 14336], P('dp', 'tensor')
Inputs may be any that keep to these rules, and one draw needn't show every extreme that they name: `packing`: each entry is g * 8 + b for a data group g and block b; the blocks named for group g are exactly its blocks 0 to count - 1, each once; a reference group takes at most one block from any data group; one data group has all 8 of its blocks named. mix_ratio[1] is 32 and mix_ratio[0] lies between 1 and 31.
All inputs are finite; a program needn't handle non-finite values.
Results may differ from a plain program's by a relative error of at most 0.02.
Values may be sent and summed in bfloat16 or wider, within the bound.
A program may use at most 256 MiB of HBM per device.

v0:
```python
import math

import jax
import jax.numpy as jnp
from jax import lax
from jax.sharding import PartitionSpec as P

BLOCK = 128


def blend_into(policy_part, old_part, weight_ratio):
    mixed = weight_ratio * policy_part.astype(jnp.float32) + (1.0 - weight_ratio) * old_part.astype(
        jnp.float32
    )
    return mixed.astype(jnp.bfloat16)


def rounded_parts(columns, weight_rows, row_width):
    pieces = weight_rows.shape[0] // row_width
    split_cols = columns.reshape(columns.shape[0], pieces, row_width)
    split_rows = weight_rows.reshape(pieces, row_width, weight_rows.shape[1])
    parts = jnp.einsum("rkw,kwf->krf", split_cols, split_rows, preferred_element_type=jnp.float32)
    return jnp.sum(parts.astype(jnp.bfloat16).astype(jnp.float32), axis=0)


def body(
    tokens, packing, tail_tokens, mix_ratio, policy_gate, policy_up, reference_gate, reference_up
):
    weight_ratio = mix_ratio[0].astype(jnp.float32) / mix_ratio[1].astype(jnp.float32)
    relaid = (
        lax.all_to_all(policy_gate, "tensor", split_axis=1, concat_axis=0, tiled=True),
        lax.all_to_all(policy_up, "tensor", split_axis=1, concat_axis=0, tiled=True),
    )
    new_gate = blend_into(relaid[0], reference_gate, weight_ratio)
    new_up = blend_into(relaid[1], reference_up, weight_ratio)
    groups = packing.shape[0]
    slot_count = packing.shape[1]
    per_group = tokens.shape[0]
    my_group = lax.axis_index("dp")
    source = packing // groups
    group_ids = jnp.arange(groups, dtype=jnp.int32)
    counts = jnp.sum((source.reshape(-1)[:, None] == group_ids[None, :]).astype(jnp.int32), axis=0)
    row_limit = (counts[my_group] - 1) * BLOCK + tail_tokens[my_group]
    keep_mask = jnp.arange(per_group, dtype=jnp.int32) < row_limit
    masked_rows = jnp.where(keep_mask[:, None], tokens, jnp.zeros((), jnp.bfloat16))
    blocks = masked_rows.reshape(groups, BLOCK, tokens.shape[1])
    from_here = source == my_group
    chosen = jnp.sum(jnp.where(from_here, packing % groups, 0), axis=1)
    present = jnp.any(from_here, axis=1)
    outgoing = jnp.where(
        present[:, None, None], jnp.take(blocks, chosen, axis=0), jnp.zeros((), jnp.bfloat16)
    )
    arrived = lax.all_to_all(outgoing, "dp", split_axis=0, concat_axis=0, tiled=True)
    packed = jnp.take(arrived, source[my_group], axis=0).reshape(
        slot_count * BLOCK, tokens.shape[1]
    )
    full_rows = lax.all_gather(packed, "tensor", axis=1, tiled=True)
    inv_width = 1.0 / math.sqrt(full_rows.shape[1])
    row_width = new_gate.shape[0]
    gate_part = rounded_parts(
        full_rows, lax.all_gather(new_gate, "dp", axis=0, tiled=True), row_width
    )
    up_part = rounded_parts(full_rows, lax.all_gather(new_up, "dp", axis=0, tiled=True), row_width)
    gate_sum = gate_part
    up_sum = up_part
    gate_sum = gate_sum * inv_width
    up_sum = up_sum * inv_width
    hidden = (jax.nn.silu(gate_sum) * up_sum).astype(jnp.bfloat16)
    return (new_gate, new_up, hidden)


def solution(mesh):
    in_specs = (
        P("dp", "tensor"),
        P(),
        P(),
        P(),
        P(("dp", "tensor"), None),
        P(("dp", "tensor"), None),
        P("dp", "tensor"),
        P("dp", "tensor"),
    )
    out_specs = (P("dp", "tensor"), P("dp", "tensor"), P("dp", "tensor"))
    return jax.shard_map(body, mesh=mesh, in_specs=in_specs, out_specs=out_specs, check_vma=False)
```

profile of v0, /device:TPU:26, one launch (start us, length us, event | category | flops | bytes accessed | tf_op | source)
XLA Modules:
  0.0 1073.2 jit_solution(16430580423133515857)
XLA Ops:
  7.2 0.8 fusion.8
  8.0 0.8 fusion.3
  8.8 0.1 eq.25
  8.9 0.1 convert_reduce_fusion.2
  9.0 1.2 dynamic_slice.11
  10.2 0.6 dynamic_slice.10
  12.2 4.6 broadcast_select_fusion
  16.7 5.0 gather_fusion
  21.7 4.7 select_select_fusion
  26.5 5.0 all-to-all-start.2
  31.4 0.0 all-gather.4.cloned.1.call-start
  31.5 0.1 broadcast_bitcast_fusion
  31.5 47.6 %all-to-all-done.2 = bf16[8,128,2048]{2,1,0:T(8,128)(2,1)} async-done(((bf16[8,128,2048]{2,1,0:T(8,128)(2,1)}), bf16[8,128,2048]{2,1,0:T(8,128)(2,1)}, u32[]{:S(2)}, u32[]{:S(2)}) %all-to-all-start.2) | async-done | bytes 4194336 | tf_op jit(solution)/shard_map/all_to_all | solution.py:53
  79.1 2.9 gather_fusion.1
  82.1 2.2 bitcast_select_fusion
  84.3 0.0 all-gather.4.cloned.1.call-update
  84.3 6.8 copy.34
  91.1 0.0 copy-start
  91.1 5.9 all-to-all-start
  97.0 0.0 all-gather.6.cloned.1.call-start
  97.1 0.0 copy-done
  97.1 0.6 fusion.9
  98.9 335.7 %all-to-all-done = bf16[256,4,3584]{2,0,1:T(8,128)(2,1)} async-done(((bf16[256,4,3584]{2,0,1:T(8,128)(2,1)}), bf16[256,4,3584]{2,0,1:T(8,128)(2,1)}, u32[]{:S(2)}, u32[]{:S(2)}) %all-to-all-start) | async-done | bytes 7340064 | tf_op jit(solution)/shard_map/all_to_all | solution.py:31
  434.6 10.3 convert_multiply_fusion.1
  444.9 10.6 fusion.1
  455.5 0.0 all-gather.6.cloned.1.call-update
  455.5 0.0 all-gather.8.cloned.1.call-start
  455.6 3.8 copy.33
  459.3 0.0 slice-start
  459.3 165.4 %all_to_all.31 = bf16[256,4,3584]{2,0,1:T(8,128)(2,1)} all-to-all(bf16[256,4,3584]{2,0,1:T(8,128)(2,1)S(1)} %bitcast.45), channel_id=1, replica_groups=mesh['dp'=8,'tensor'=4] {'tensor'}, dimensions={1} | all-to-all | bytes 14680064 | tf_op jit(solution)/shard_map/all_to_all | solution.py:32
  624.7 0.0 slice-start.1
  624.7 10.7 convert_multiply_fusion
  635.4 0.0 slice-done
  635.4 0.0 slice-done.1
  635.4 8.6 fusion
  644.0 0.0 all-gather.8.cloned.1.call-update
  644.1 0.0 all-gather.4.cloned.1.call-done
  644.1 15.9 %copy.24 = bf16[768,8192]{0,1:T(8,128)(2,1)} copy(bf16[768,8192]{1,0:T(8,128)(2,1)} %all-gather.4.cloned.1.call-done) | data formatting | bytes 25165824 | tf_op jit(solution)/shard_map/all_gather | solution.py:57
  660.0 67.7 %all-gather.6.cloned.1.call-done = bf16[8192,3584]{1,0:T(8,128)(2,1)} async-done(((bf16[1024,3584]{1,0:T(8,128)(2,1)}), bf16[8192,3584]{1,0:T(8,128)(2,1)}) %all-gather.6.cloned.1.call-update) | async-done | bytes 58720272 | tf_op jit(solution)/shard_map/all_gather | solution.py:61
  727.7 58.4 %convert_reduce_fusion.1 = f32[768,3584]{1,0:T(8,128)} fusion(bf16[768,8,1024]{0,2,1:T(8,128)(2,1)} %bitcast.47, bf16[8,1024,3584]{2,1,0:T(8,128)(2,1)} %bitcast.53), kind=kOutput, calls=%fused_computation.3 | convolution fusion | flops 45160464384 | bytes 82313216 | tf_op jit(solution)/shard_map/rkw,kwf->krf/dot_general | solution.py:22
  786.1 211.5 %all-gather.8.cloned.1.call-done = bf16[8192,3584]{1,0:T(8,128)(2,1)} async-done(((bf16[1024,3584]{1,0:T(8,128)(2,1)}), bf16[8192,3584]{1,0:T(8,128)(2,1)}) %all-gather.8.cloned.1.call-update) | async-done | bytes 58720272 | tf_op jit(solution)/shard_map/all_gather | solution.py:63
  997.6 57.7 %convert_reduce_fusion = f32[768,3584]{1,0:T(8,128)} fusion(bf16[768,8,1024]{0,2,1:T(8,128)(2,1)} %bitcast.48, bf16[8,1024,3584]{2,1,0:T(8,128)(2,1)} %bitcast.54), kind=kOutput, calls=%fused_computation.2 | convolution fusion | flops 45160464384 | bytes 82313216 | tf_op jit(solution)/shard_map/rkw,kwf->krf/dot_general | solution.py:22
  1055.3 11.3 %multiply_convert_fusion = bf16[768,3584]{1,0:T(8,128)(2,1)} fusion(f32[768,3584]{1,0:T(8,128)} %convert_reduce_fusion, f32[768,3584]{1,0:T(8,128)} %convert_reduce_fusion.1), kind=kLoop, calls=%fused_computation.10 | loop fusion | flops 22020096 | bytes 27525120 | tf_op jit(solution)/shard_map/convert_element_type | solution.py:68
  (8 shorter events, 0.1 us)
Async XLA Ops:
  26.5 52.7 %all-to-all-start.2 = ((bf16[8,128,2048]{2,1,0:T(8,128)(2,1)}), bf16[8,128,2048]{2,1,0:T(8,128)(2,1)}, u32[]{:S(2)}, u32[]{:S(2)}) async-start(bf16[8,128,2048]{2,1,0:T(8,128)(2,1)} %select_select_fusion), calls=%async_computation.2 | async-start | bytes 8388608 | tf_op jit(solution)/shard_map/all_to_all | solution.py:53
  31.4 612.7 %all-gather.4.cloned.1.call-start = ((), (), s32[]{:S(2)}) async-start(), calls=%async_computation.3 | async-start | bytes 15728640 | tf_op jit(solution)/shard_map/all_gather | solution.py:57
  91.1 5.9 copy-start
  91.1 343.5 %all-to-all-start = ((bf16[256,4,3584]{2,0,1:T(8,128)(2,1)}), bf16[256,4,3584]{2,0,1:T(8,128)(2,1)}, u32[]{:S(2)}, u32[]{:S(2)}) async-start(bf16[256,4,3584]{2,0,1:T(8,128)(2,1)} %bitcast.44), calls=%async_computation | async-start | bytes 14680064 | tf_op jit(solution)/shard_map/all_to_all | solution.py:31
  97.0 630.7 %all-gather.6.cloned.1.call-start = ((), (), s32[]{:S(2)}) async-start(), calls=%async_computation.4 | async-start | bytes 66060288 | tf_op jit(solution)/shard_map/all_gather | solution.py:61
  455.5 542.1 %all-gather.8.cloned.1.call-start = ((), (), s32[]{:S(2)}) async-start(), calls=%async_computation.5 | async-start | bytes 66060288 | tf_op jit(solution)/shard_map/all_gather | solution.py:63
  459.3 176.1 %slice-start = ((s8[7340032]{0:T(1024)(128)(4,1)}), s8[3145728]{0:T(1024)(128)(4,1)S(1)}, s32[]{:S(2)}) async-start(s8[7340032]{0:T(1024)(128)(4,1)} %bitcast.51), calls=%async_computation.6 | async-start | bytes 6291456
  624.7 10.7 slice-start.1
Sparse Core Ops, SparseCore 0:
  84.4 372.8 all-gather.3
  459.8 267.8 all-gather.5
  730.2 267.3 all-gather.7
where the time goes:
time: 1080 us; the launch traced here: 1070 us
  waiting for transfers between devices  663 us (61%)
  blocking collectives  165 us (15%)
  matrix products  116 us (11%)
  other arithmetic  64.8 us (6%)
  local copies, waits for them, and re-layouts  37 us (3%)
  between operations  16.4 us (2%)
  starting transfers between devices  10.9 us (1%)
    all_to_all x1, waiting for transfers between devices, body(): lax.all_to_all(policy_gate, 'tensor', split_axis=1, concat_axis=0, tiled=...  336 us
    all_gather x1, waiting for transfers between devices, body(): lax.all_gather(new_up, 'dp', axis=0, tiled=True)  212 us
    all_to_all x1, blocking collectives, body(): lax.all_to_all(policy_up, 'tensor', split_axis=1, concat_axis=0, tiled=True)  165 us
    dot_general x2, matrix products, rounded_parts(): jnp.einsum('rkw,kwf->krf', split_cols, split_rows, preferred_element_type...  116 us
    all_gather x1, waiting for transfers between devices, body(): lax.all_gather(new_gate, 'dp', axis=0, tiled=True)  67.7 us
    all_to_all x1, waiting for transfers between devices, body(): lax.all_to_all(outgoing, 'dp', split_axis=0, concat_axis=0, tiled=True)  47.6 us
  transfers between devices with their start and end apart: 5, of which 4 were waited for; matrix products, arithmetic and copies ran while one was open for 12% of the time, Pallas kernels for 0%

commit v1 on v0

v1 whole, which is shorter than its diff:
```python
import math

import jax
import jax.numpy as jnp
from jax import lax
from jax.sharding import PartitionSpec as P

BLOCK = 128
UNITS = 28
CHUNKS = (4, 8, 8, 8)


def blend_into(policy_part, old_part, weight_ratio):
    mixed = weight_ratio * policy_part.astype(jnp.float32) + (1.0 - weight_ratio) * old_part.astype(
        jnp.float32
    )
    return mixed.astype(jnp.bfloat16)


def shift_perm(count, shift):
    return [(i, (i + shift) % count) for i in range(count)]


def body(
    tokens, packing, tail_tokens, mix_ratio, policy_gate, policy_up, reference_gate, reference_up
):
    weight_ratio = mix_ratio[0].astype(jnp.float32) / mix_ratio[1].astype(jnp.float32)
    planes = lax.axis_size("tensor")
    my_plane = lax.axis_index("tensor")
    rows = policy_gate.shape[0]
    width = reference_gate.shape[1]

    pieces = []
    edge = 0
    for units in CHUNKS:
        cols = width * units // UNITS
        chunk = []
        for policy in (policy_gate, policy_up):
            got = []
            for shift in range(planes):
                target = lax.rem(my_plane + shift, planes)
                piece = lax.dynamic_slice(policy, (0, target * width + edge), (rows, cols))
                if shift:
                    piece = lax.ppermute(piece, "tensor", shift_perm(planes, shift))
                got.append(piece)
            chunk.append(got)
        pieces.append((edge, cols, chunk))
        edge += cols

    groups = packing.shape[0]
    slot_count = packing.shape[1]
    per_group = tokens.shape[0]
    feats = tokens.shape[1]
    my_group = lax.axis_index("dp")
    source = packing // groups
    group_ids = jnp.arange(groups, dtype=jnp.int32)
    counts = jnp.sum((source.reshape(-1)[:, None] == group_ids[None, :]).astype(jnp.int32), axis=0)
    row_limit = (counts[my_group] - 1) * BLOCK + tail_tokens[my_group]
    blocks = tokens.reshape(per_group // BLOCK, BLOCK, feats)
    from_here = source == my_group
    chosen = jnp.sum(jnp.where(from_here, packing % groups, 0), axis=1)
    block_row = jnp.arange(BLOCK, dtype=jnp.int32)
    keep = (chosen[:, None] * BLOCK + block_row[None, :]) < row_limit
    outgoing = jnp.where(keep[:, :, None], jnp.take(blocks, chosen, axis=0), jnp.zeros((), jnp.bfloat16))
    arrived = lax.all_to_all(outgoing, "dp", split_axis=0, concat_axis=0, tiled=True)
    packed = jnp.take(arrived, source[my_group], axis=0).reshape(slot_count * BLOCK, feats)
    full_rows = jnp.zeros((slot_count * BLOCK, feats * planes), jnp.bfloat16)
    for shift in range(planes):
        origin = lax.rem(my_plane + planes - shift, planes)
        part = packed if shift == 0 else lax.ppermute(packed, "tensor", shift_perm(planes, shift))
        full_rows = lax.dynamic_update_slice(full_rows, part, (0, origin * feats))

    inv_width = 1.0 / math.sqrt(full_rows.shape[1])
    new_parts = ([], [])
    hidden_parts = []
    for edge, cols, chunk in pieces:
        sums = []
        for which, (old, got) in enumerate(zip((reference_gate, reference_up), chunk)):
            new = jnp.zeros((rows * planes, cols), jnp.bfloat16)
            for shift in range(planes):
                origin = lax.rem(my_plane + planes - shift, planes)
                old_part = lax.dynamic_slice(old, (origin * rows, edge), (rows, cols))
                new = lax.dynamic_update_slice(
                    new, blend_into(got[shift], old_part, weight_ratio), (origin * rows, 0)
                )
            new_parts[which].append(new)
            gathered = lax.all_gather(new, "dp", axis=0, tiled=True)
            sums.append(jnp.dot(full_rows, gathered, preferred_element_type=jnp.float32) * inv_width)
        hidden_parts.append((jax.nn.silu(sums[0]) * sums[1]).astype(jnp.bfloat16))
    return (
        jnp.concatenate(new_parts[0], axis=1),
        jnp.concatenate(new_parts[1], axis=1),
        jnp.concatenate(hidden_parts, axis=1),
    )


def solution(mesh):
    in_specs = (
        P("dp", "tensor"),
        P(),
        P(),
        P(),
        P(("dp", "tensor"), None),
        P(("dp", "tensor"), None),
        P("dp", "tensor"),
        P("dp", "tensor"),
    )
    out_specs = (P("dp", "tensor"), P("dp", "tensor"), P("dp", "tensor"))
    return jax.shard_map(body, mesh=mesh, in_specs=in_specs, out_specs=out_specs, check_vma=False)
```

time: 1080 us -> 935 us (0.87)
  blocking collectives: 165 us -> 0 us
  waiting for transfers between devices: 663 us -> 574 us
  starting transfers between devices: 10.9 us -> 74.3 us
  matrix products: 116 us -> 151 us
    ppermute x0 -> x27, waiting for transfers between devices: none -> 531 us  [the longest x24 277 us: body(): piece = lax.ppermute(piece, 'tensor', shift_perm(planes, shift))]
    all_to_all x1 -> x0, waiting for transfers between devices: 336 us -> none  [body(): lax.all_to_all(policy_gate, 'tensor', split_axis=1, concat_axis=0, tiled=...]
    all_gather x3 -> x8, waiting for transfers between devices: 279 us -> 0.05 us  [body(): gathered = lax.all_gather(new, 'dp', axis=0, tiled=True)]
    all_to_all x1 -> x0, blocking collectives: 165 us -> none  [body(): lax.all_to_all(policy_up, 'tensor', split_axis=1, concat_axis=0, tiled=True)]
    ppermute x0 -> x27, starting transfers between devices: none -> 68.9 us  [the longest x24 66.3 us: body(): piece = lax.ppermute(piece, 'tensor', shift_perm(planes, shift))]
    dot_general x2 -> x8, matrix products: 116 us -> 151 us  [body(): jnp.dot(full_rows, gathered, preferred_element_type=jnp.float32) * inv_width]
    convert_element_type x3 -> x0, other arithmetic: 30.5 us -> none  [the longest x2 19.1 us: blend_into(): return mixed.astype(jnp.bfloat16)]
    dynamic_update_slice x0 -> x13, other arithmetic: none -> 23.5 us  [the longest x12 20 us: body(): lax.dynamic_update_slice(new, blend_into(got[shift], old_part, weight_rat...]
  transfers between devices with their start and end apart: 5 -> 36, of which waited for: 4 -> 20; matrix products, arithmetic and copies ran while one was open for 12% -> 24% of each run, Pallas kernels for 0% -> 0%
where the time goes in v1:
time: 935 us; the launch traced here: 926 us
  waiting for transfers between devices  574 us (61%)
  matrix products  151 us (16%)
  starting transfers between devices  74.3 us (8%)
  other arithmetic  64.6 us (7%)
  local copies, waits for them, and re-layouts  44.1 us (5%)
  between operations  17.7 us (2%)
    ppermute x24, waiting for transfers between devices, body(): piece = lax.ppermute(piece, 'tensor', shift_perm(planes, shift))  277 us
    ppermute x3, waiting for transfers between devices, body(): lax.ppermute(packed, 'tensor', shift_perm(planes, shift))  254 us
    dot_general x8, matrix products, body(): jnp.dot(full_rows, gathered, preferred_element_type=jnp.float32) * inv_width  151 us
    ppermute x24, starting transfers between devices, body(): piece = lax.ppermute(piece, 'tensor', shift_perm(planes, shift))  66.3 us
    all_to_all x1, waiting for transfers between devices, body(): lax.all_to_all(outgoing, 'dp', split_axis=0, concat_axis=0, tiled=True)  42.7 us
    dynamic_slice x8, other arithmetic, body(): piece = lax.dynamic_slice(policy, (0, target * width + edge), (rows, cols))  22.7 us
    dynamic_update_slice x12, other arithmetic, body(): lax.dynamic_update_slice(new, blend_into(got[shift], old_part, weight_rat...  20 us
  transfers between devices with their start and end apart: 36, of which 20 were waited for; matrix products, arithmetic and copies ran while one was open for 24% of the time, Pallas kernels for 0%

profile of v1, /device:TPU:26, one launch (start us, length us, event | category | flops | bytes accessed | tf_op | source)
XLA Modules:
  0.0 926.3 jit_solution(2344778474672298142)
XLA Ops:
  13.8 6.1 collective-permute-done
  21.0 15.3 %collective-permute-done.1 = bf16[256,512]{1,0:T(8,128)(2,1)S(1)} collective-permute-done((bf16[256,512]{1,0:T(8,128)(2,1)S(1)}, bf16[256,512]{1,0:T(8,128)(2,1)S(1)}, u32[]{:S(2)}, u32[]{:S(2)}) %collective-permute-start.1) | collective-permute-done | bytes 262176 | tf_op jit(solution)/shard_map/ppermute | solution.py:44
  43.3 5.5 collective-permute-done.12
  49.9 14.7 %collective-permute-done.13 = bf16[256,512]{1,0:T(8,128)(2,1)S(1)} collective-permute-done((bf16[256,512]{1,0:T(8,128)(2,1)S(1)}, bf16[256,512]{1,0:T(8,128)(2,1)S(1)}, u32[]{:S(2)}, u32[]{:S(2)}) %collective-permute-start.13) | collective-permute-done | bytes 262176 | tf_op jit(solution)/shard_map/ppermute | solution.py:44
  72.4 13.2 %collective-permute-done.3 = bf16[256,1024]{1,0:T(8,128)(2,1)S(1)} collective-permute-done((bf16[256,1024]{1,0:T(8,128)(2,1)S(1)}, bf16[256,1024]{1,0:T(8,128)(2,1)S(1)}, u32[]{:S(2)}, u32[]{:S(2)}) %collective-permute-start.3) | collective-permute-done | bytes 524320 | tf_op jit(solution)/shard_map/ppermute | solution.py:44
  85.9 3.2 constant_dynamic-slice_fusion.19
  91.3 23.1 %collective-permute-done.4 = bf16[256,1024]{1,0:T(8,128)(2,1)S(1)} collective-permute-done((bf16[256,1024]{1,0:T(8,128)(2,1)}, bf16[256,1024]{1,0:T(8,128)(2,1)S(1)}, u32[]{:S(2)}, u32[]{:S(2)}) %collective-permute-start.4) | collective-permute-done | bytes 524320 | tf_op jit(solution)/shard_map/ppermute | solution.py:44
  116.8 4.8 constant_dynamic-slice_fusion.18
  121.6 11.3 %collective-permute-start.5 = (bf16[256,1024]{1,0:T(8,128)(2,1)S(1)}, bf16[256,1024]{1,0:T(8,128)(2,1)S(1)}, u32[]{:S(2)}, u32[]{:S(2)}) collective-permute-start(bf16[256,1024]{1,0:T(8,128)(2,1)S(1)} %get-tuple-element.34), channel_id=1, source_target_pairs={{0,3},{1,0},{2,1},{3,2},{4,7},{5,4},{6,5},{7,6},{8,11},{9,8},{10,9... | collective-permute-start | bytes 1572872 | tf_op jit(solution)/shard_map/ppermute | solution.py:44
  135.2 12.1 %collective-permute-done.5 = bf16[256,1024]{1,0:T(8,128)(2,1)S(1)} collective-permute-done((bf16[256,1024]{1,0:T(8,128)(2,1)S(1)}, bf16[256,1024]{1,0:T(8,128)(2,1)S(1)}, u32[]{:S(2)}, u32[]{:S(2)}) %collective-permute-start.5) | collective-permute-done | bytes 524320 | tf_op jit(solution)/shard_map/ppermute | solution.py:44
  147.4 21.2 %collective-permute-done.7 = bf16[256,1024]{1,0:T(8,128)(2,1)S(1)} collective-permute-done((bf16[256,1024]{1,0:T(8,128)(2,1)S(1)}, bf16[256,1024]{1,0:T(8,128)(2,1)S(1)}, u32[]{:S(2)}, u32[]{:S(2)}) %collective-permute-start.7) | collective-permute-done | bytes 524320 | tf_op jit(solution)/shard_map/ppermute | solution.py:44
  168.6 3.1 fusion.3
  174.0 12.0 %collective-permute-start.15 = (bf16[256,1024]{1,0:T(8,128)(2,1)S(1)}, bf16[256,1024]{1,0:T(8,128)(2,1)S(1)}, u32[]{:S(2)}, u32[]{:S(2)}) collective-permute-start(bf16[256,1024]{1,0:T(8,128)(2,1)S(1)} %get-tuple-element.23), channel_id=1, source_target_pairs={{0,1},{1,2},{2,3},{3,0},{4,5},{5,6},{6,7},{7,4},{8,9},{9,10},{10,1... | collective-permute-start | bytes 1572872 | tf_op jit(solution)/shard_map/ppermute | solution.py:44
  186.0 11.8 %collective-permute-done.15 = bf16[256,1024]{1,0:T(8,128)(2,1)S(1)} collective-permute-done((bf16[256,1024]{1,0:T(8,128)(2,1)S(1)}, bf16[256,1024]{1,0:T(8,128)(2,1)S(1)}, u32[]{:S(2)}, u32[]{:S(2)}) %collective-permute-start.15) | collective-permute-done | bytes 524320 | tf_op jit(solution)/shard_map/ppermute | solution.py:44
  201.4 3.3 collective-permute-start.18
  204.7 22.5 %collective-permute-done.16 = bf16[256,1024]{1,0:T(8,128)(2,1)S(1)} collective-permute-done((bf16[256,1024]{1,0:T(8,128)(2,1)S(1)}, bf16[256,1024]{1,0:T(8,128)(2,1)S(1)}, u32[]{:S(2)}, u32[]{:S(2)}) %collective-permute-start.16) | collective-permute-done | bytes 524320 | tf_op jit(solution)/shard_map/ppermute | solution.py:44
  227.4 4.7 constant_dynamic-slice_fusion.6
  232.1 10.8 %collective-permute-start.17 = (bf16[256,1024]{1,0:T(8,128)(2,1)S(1)}, bf16[256,1024]{1,0:T(8,128)(2,1)S(1)}, u32[]{:S(2)}, u32[]{:S(2)}) collective-permute-start(bf16[256,1024]{1,0:T(8,128)(2,1)S(1)} %get-tuple-element.10), channel_id=1, source_target_pairs={{0,3},{1,0},{2,1},{3,2},{4,7},{5,4},{6,5},{7,6},{8,11},{9,8},{10,9... | collective-permute-start | bytes 1572872 | tf_op jit(solution)/shard_map/ppermute | solution.py:44
  245.3 11.2 %collective-permute-done.17 = bf16[256,1024]{1,0:T(8,128)(2,1)S(1)} collective-permute-done((bf16[256,1024]{1,0:T(8,128)(2,1)S(1)}, bf16[256,1024]{1,0:T(8,128)(2,1)S(1)}, u32[]{:S(2)}, u32[]{:S(2)}) %collective-permute-start.17) | collective-permute-done | bytes 524320 | tf_op jit(solution)/shard_map/ppermute | solution.py:44
  256.5 21.7 %collective-permute-done.19 = bf16[256,1024]{1,0:T(8,128)(2,1)S(1)} collective-permute-done((bf16[256,1024]{1,0:T(8,128)(2,1)S(1)}, bf16[256,1024]{1,0:T(8,128)(2,1)S(1)}, u32[]{:S(2)}, u32[]{:S(2)}) %collective-permute-start.19) | collective-permute-done | bytes 524320 | tf_op jit(solution)/shard_map/ppermute | solution.py:44
  283.0 10.7 %collective-permute-start.10 = (bf16[256,1024]{1,0:T(8,128)(2,1)}, bf16[256,1024]{1,0:T(8,128)(2,1)S(1)}, u32[]{:S(2)}, u32[]{:S(2)}) collective-permute-start(bf16[256,1024]{1,0:T(8,128)(2,1)} %get-tuple-element.42), channel_id=1, source_target_pairs={{0,2},{1,3},{2,0},{3,1},{4,6},{5,7},{6,4},{7,5},{8,10},{9,11},{10,... | collective-permute-start | bytes 1572872 | tf_op jit(solution)/shard_map/ppermute | solution.py:44
  296.0 32.6 %collective-permute-done.10 = bf16[256,1024]{1,0:T(8,128)(2,1)S(1)} collective-permute-done((bf16[256,1024]{1,0:T(8,128)(2,1)}, bf16[256,1024]{1,0:T(8,128)(2,1)S(1)}, u32[]{:S(2)}, u32[]{:S(2)}) %collective-permute-start.10) | collective-permute-done | bytes 524320 | tf_op jit(solution)/shard_map/ppermute | solution.py:44
  334.0 14.3 %collective-permute-done.20 = bf16[256,1024]{1,0:T(8,128)(2,1)S(1)} collective-permute-done((bf16[256,1024]{1,0:T(8,128)(2,1)}, bf16[256,1024]{1,0:T(8,128)(2,1)S(1)}, u32[]{:S(2)}, u32[]{:S(2)}) %collective-permute-start.20) | collective-permute-done | bytes 524320 | tf_op jit(solution)/shard_map/ppermute | solution.py:44
  348.3 20.8 %collective-permute-done.22 = bf16[256,1024]{1,0:T(8,128)(2,1)S(1)} collective-permute-done((bf16[256,1024]{1,0:T(8,128)(2,1)}, bf16[256,1024]{1,0:T(8,128)(2,1)S(1)}, u32[]{:S(2)}, u32[]{:S(2)}) %collective-permute-start.22) | collective-permute-done | bytes 524320 | tf_op jit(solution)/shard_map/ppermute | solution.py:44
  372.2 15.5 %collective-permute-done.11 = bf16[256,1024]{1,0:T(8,128)(2,1)S(1)} collective-permute-done((bf16[256,1024]{1,0:T(8,128)(2,1)S(1)}, bf16[256,1024]{1,0:T(8,128)(2,1)S(1)}, u32[]{:S(2)}, u32[]{:S(2)}) %collective-permute-start.11) | collective-permute-done | bytes 524320 | tf_op jit(solution)/shard_map/ppermute | solution.py:44
  392.7 5.8 gather_fusion
  398.6 3.9 select_select_fusion
  402.5 5.1 all-to-all-start
  407.7 15.7 %collective-permute-done.23 = bf16[256,1024]{1,0:T(8,128)(2,1)S(1)} collective-permute-done((bf16[256,1024]{1,0:T(8,128)(2,1)S(1)}, bf16[256,1024]{1,0:T(8,128)(2,1)S(1)}, u32[]{:S(2)}, u32[]{:S(2)}) %collective-permute-start.23) | collective-permute-done | bytes 524320 | tf_op jit(solution)/shard_map/ppermute | solution.py:44
  426.1 42.7 %all-to-all-done = bf16[8,128,2048]{2,1,0:T(8,128)(2,1)} async-done(((bf16[8,128,2048]{2,1,0:T(8,128)(2,1)}), bf16[8,128,2048]{2,1,0:T(8,128)(2,1)}, u32[]{:S(2)}, u32[]{:S(2)}) %all-to-all-start) | async-done | bytes 4194336 | tf_op jit(solution)/shard_map/all_to_all | solution.py:65
  468.8 4.7 gather_fusion.1
  473.5 6.1 broadcast_in_dim.45
  479.6 3.4 constant_dynamic-update-slice_fusion.2
  485.6 5.9 pad_maximum_fusion.1
  491.5 5.6 pad_maximum_fusion
  497.1 56.4 %collective-permute-done.24 = bf16[768,2048]{1,0:T(8,128)(2,1)} collective-permute-done((bf16[768,2048]{1,0:T(8,128)(2,1)}, bf16[768,2048]{1,0:T(8,128)(2,1)}, u32[]{:S(2)}, u32[]{:S(2)}) %collective-permute-start.24) | collective-permute-done | bytes 3145760 | tf_op jit(solution)/shard_map/ppermute | solution.py:70
  553.5 4.4 constant_dynamic-update-slice_fusion.3
  557.9 197.5 %collective-permute-done.25 = bf16[768,2048]{1,0:T(8,128)(2,1)} collective-permute-done((bf16[768,2048]{1,0:T(8,128)(2,1)}, bf16[768,2048]{1,0:T(8,128)(2,1)}, u32[]{:S(2)}, u32[]{:S(2)}) %collective-permute-start.25) | collective-permute-done | bytes 3145760 | tf_op jit(solution)/shard_map/ppermute | solution.py:70
  755.4 4.0 constant_dynamic-update-slice_fusion.1
  759.4 4.0 constant_dynamic-update-slice_fusion
  763.4 14.2 %convolution_multiply_fusion.1 = f32[768,512]{0,1:T(8,128)S(1)} fusion(bf16[768,8192]{1,0:T(8,128)(2,1)} %constant_dynamic-update-slice_fusion, bf16[8192,512]{1,0:T(8,128)(2,1)} %all-gather.9.cloned.1.call-done), kind=kOutput, calls=%fused_computation.11 | convolution fusion | flops 6442844160 | bytes 22544384 | tf_op jit(solution)/shard_map/dot_general | solution.py:88
  777.6 11.4 %multiply_convert_fusion.3 = bf16[768,512]{0,1:T(8,128)(2,1)S(1)} fusion(f32[768,512]{0,1:T(8,128)S(1)} %convolution_multiply_fusion.1, bf16[768,8192]{1,0:T(8,128)(2,1)} %constant_dynamic-update-slice_fusion, bf16[8192,512]{1,0:T(8,128)(2,1)} %all-gather.11.cloned.1.call-done), kind=kOutput, calls=%fused_computation.12 | convolution fusion | flops 6445203456 | bytes 23330816 | tf_op jit(solution)/shard_map/dot_general | solution.py:88
  790.2 20.3 %fusion.39 = f32[768,1024]{1,0:T(8,128)} fusion(bf16[768,8192]{1,0:T(8,128)(2,1)} %constant_dynamic-update-slice_fusion, bf16[8192,1024]{1,0:T(8,128)(2,1)} %all-gather.13.cloned.1.call-done), kind=kOutput, calls=%fused_computation.132 | convolution fusion | flops 12884901888 | bytes 32505856 | tf_op jit(solution)/shard_map/dot_general | solution.py:88
  810.6 21.3 %multiply_convert_fusion.2 = bf16[768,1024]{1,0:T(8,128)(2,1)S(1)} fusion(f32[768,1024]{1,0:T(8,128)} %fusion.39, bf16[768,8192]{1,0:T(8,128)(2,1)} %constant_dynamic-update-slice_fusion, bf16[8192,1024]{1,0:T(8,128)(2,1)} %all-gather.15.cloned.1.call-done), kind=kOutput, calls=%fused_computation.9 | convolution fusion | flops 12891193344 | bytes 34078720 | tf_op jit(solution)/shard_map/dot_general | solution.py:88
  831.9 20.4 %fusion.40 = f32[768,1024]{1,0:T(8,128)} fusion(bf16[768,8192]{1,0:T(8,128)(2,1)} %constant_dynamic-update-slice_fusion, bf16[8192,1024]{1,0:T(8,128)(2,1)} %all-gather.17.cloned.1.call-done), kind=kOutput, calls=%fused_computation.133 | convolution fusion | flops 12884901888 | bytes 32505856 | tf_op jit(solution)/shard_map/dot_general | solution.py:88
  852.3 22.2 %multiply_convert_fusion.1 = bf16[768,1024]{1,0:T(8,128)(2,1)} fusion(f32[768,1024]{1,0:T(8,128)} %fusion.40, bf16[768,8192]{1,0:T(8,128)(2,1)} %constant_dynamic-update-slice_fusion, bf16[8192,1024]{1,0:T(8,128)(2,1)} %all-gather.19.cloned.1.call-done), kind=kOutput, calls=%fused_computation.8 | convolution fusion | flops 12891193344 | bytes 34078720 | tf_op jit(solution)/shard_map/dot_general | solution.py:88
  874.4 20.4 %fusion.41 = f32[768,1024]{1,0:T(8,128)} fusion(bf16[768,8192]{1,0:T(8,128)(2,1)} %constant_dynamic-update-slice_fusion, bf16[8192,1024]{1,0:T(8,128)(2,1)} %all-gather.21.cloned.1.call-done), kind=kOutput, calls=%fused_computation.134 | convolution fusion | flops 12884901888 | bytes 32505856 | tf_op jit(solution)/shard_map/dot_general | solution.py:88
  894.9 21.4 %multiply_convert_fusion = bf16[768,1024]{1,0:T(8,128)(2,1)S(1)} fusion(f32[768,1024]{1,0:T(8,128)} %fusion.41, bf16[768,8192]{1,0:T(8,128)(2,1)} %constant_dynamic-update-slice_fusion, bf16[8192,1024]{1,0:T(8,128)(2,1)} %all-gather.23.cloned.1.call-done), kind=kOutput, calls=%fused_computation.7 | convolution fusion | flops 12891193344 | bytes 34078720 | tf_op jit(solution)/shard_map/dot_general | solution.py:88
  (127 shorter events, 66.4 us)
Async XLA Ops:
  7.2 756.3 %all-gather.9.cloned.1.call-start = ((), (), s32[]{:S(2)}) async-start(), calls=%async_computation.1 | async-start | bytes 9437184 | tf_op jit(solution)/shard_map/all_gather | solution.py:87
  11.4 8.5 collective-permute-start
  11.7 24.6 %collective-permute-start.1 = (bf16[256,512]{1,0:T(8,128)(2,1)S(1)}, bf16[256,512]{1,0:T(8,128)(2,1)S(1)}, u32[]{:S(2)}, u32[]{:S(2)}) collective-permute-start(bf16[256,512]{1,0:T(8,128)(2,1)S(1)} %get-tuple-element.28), channel_id=1, source_target_pairs={{0,2},{1,3},{2,0},{3,1},{4,6},{5,7},{6,4},{7,5},{8,10},{9,11},{10,... | collective-permute-start | bytes 786440 | tf_op jit(solution)/shard_map/ppermute | solution.py:44
  13.4 23.9 %collective-permute-start.2 = (bf16[256,512]{1,0:T(8,128)(2,1)S(1)}, bf16[256,512]{1,0:T(8,128)(2,1)S(1)}, u32[]{:S(2)}, u32[]{:S(2)}) collective-permute-start(bf16[256,512]{1,0:T(8,128)(2,1)S(1)} %get-tuple-element.27), channel_id=1, source_target_pairs={{0,3},{1,0},{2,1},{3,2},{4,7},{5,4},{6,5},{7,6},{8,11},{9,8},{10,9... | collective-permute-start | bytes 786440 | tf_op jit(solution)/shard_map/ppermute | solution.py:44
  39.4 738.2 %all-gather.11.cloned.1.call-start = ((), (), s32[]{:S(2)}) async-start(), calls=%async_computation.2 | async-start | bytes 9437184 | tf_op jit(solution)/shard_map/all_gather | solution.py:87
  40.9 7.9 collective-permute-start.12
  41.0 23.6 %collective-permute-start.13 = (bf16[256,512]{1,0:T(8,128)(2,1)S(1)}, bf16[256,512]{1,0:T(8,128)(2,1)S(1)}, u32[]{:S(2)}, u32[]{:S(2)}) collective-permute-start(bf16[256,512]{1,0:T(8,128)(2,1)S(1)} %get-tuple-element.4), channel_id=1, source_target_pairs={{0,2},{1,3},{2,0},{3,1},{4,6},{5,7},{6,4},{7,5},{8,10},{9,11},{10,... | collective-permute-start | bytes 786440 | tf_op jit(solution)/shard_map/ppermute | solution.py:44
  41.3 24.3 %collective-permute-start.14 = (bf16[256,512]{1,0:T(8,128)(2,1)S(1)}, bf16[256,512]{1,0:T(8,128)(2,1)S(1)}, u32[]{:S(2)}, u32[]{:S(2)}) collective-permute-start(bf16[256,512]{1,0:T(8,128)(2,1)S(1)} %get-tuple-element.3), channel_id=1, source_target_pairs={{0,3},{1,0},{2,1},{3,2},{4,7},{5,4},{6,5},{7,6},{8,11},{9,8},{10,9... | collective-permute-start | bytes 786440 | tf_op jit(solution)/shard_map/ppermute | solution.py:44
  67.7 722.5 %all-gather.13.cloned.1.call-start = ((), (), s32[]{:S(2)}) async-start(), calls=%async_computation.3 | async-start | bytes 18874368 | tf_op jit(solution)/shard_map/all_gather | solution.py:87
  72.4 13.2 %collective-permute-start.3 = (bf16[256,1024]{1,0:T(8,128)(2,1)S(1)}, bf16[256,1024]{1,0:T(8,128)(2,1)S(1)}, u32[]{:S(2)}, u32[]{:S(2)}) collective-permute-start(bf16[256,1024]{1,0:T(8,128)(2,1)S(1)} %get-tuple-element.47), channel_id=1, source_target_pairs={{0,1},{1,2},{2,3},{3,0},{4,5},{5,6},{6,7},{7,4},{8,9},{9,10},{10,1... | collective-permute-start | bytes 1572872 | tf_op jit(solution)/shard_map/ppermute | solution.py:44
  89.1 25.4 %collective-permute-start.4 = (bf16[256,1024]{1,0:T(8,128)(2,1)}, bf16[256,1024]{1,0:T(8,128)(2,1)S(1)}, u32[]{:S(2)}, u32[]{:S(2)}) collective-permute-start(bf16[256,1024]{1,0:T(8,128)(2,1)} %get-tuple-element.43), channel_id=1, source_target_pairs={{0,2},{1,3},{2,0},{3,1},{4,6},{5,7},{6,4},{7,5},{8,10},{9,11},{10,... | collective-permute-start | bytes 1572872 | tf_op jit(solution)/shard_map/ppermute | solution.py:44
  90.2 24.3 %collective-permute-start.6 = (bf16[256,1024]{1,0:T(8,128)(2,1)}, bf16[256,1024]{1,0:T(8,128)(2,1)S(1)}, u32[]{:S(2)}, u32[]{:S(2)}) collective-permute-start(bf16[256,1024]{1,0:T(8,128)(2,1)} %get-tuple-element.44), channel_id=1, source_target_pairs={{0,1},{1,2},{2,3},{3,0},{4,5},{5,6},{6,7},{7,4},{8,9},{9,10},{10,1... | collective-permute-start | bytes 1572872 | tf_op jit(solution)/shard_map/ppermute | solution.py:44
  121.6 25.8 %collective-permute-start.5 = (bf16[256,1024]{1,0:T(8,128)(2,1)S(1)}, bf16[256,1024]{1,0:T(8,128)(2,1)S(1)}, u32[]{:S(2)}, u32[]{:S(2)}) collective-permute-start(bf16[256,1024]{1,0:T(8,128)(2,1)S(1)} %get-tuple-element.34), channel_id=1, source_target_pairs={{0,3},{1,0},{2,1},{3,2},{4,7},{5,4},{6,5},{7,6},{8,11},{9,8},{10,9... | collective-permute-start | bytes 1572872 | tf_op jit(solution)/shard_map/ppermute | solution.py:44
  132.8 35.7 %collective-permute-start.7 = (bf16[256,1024]{1,0:T(8,128)(2,1)S(1)}, bf16[256,1024]{1,0:T(8,128)(2,1)S(1)}, u32[]{:S(2)}, u32[]{:S(2)}) collective-permute-start(bf16[256,1024]{1,0:T(8,128)(2,1)S(1)} %get-tuple-element.40), channel_id=1, source_target_pairs={{0,2},{1,3},{2,0},{3,1},{4,6},{5,7},{6,4},{7,5},{8,10},{9,11},{10,... | collective-permute-start | bytes 1572872 | tf_op jit(solution)/shard_map/ppermute | solution.py:44
  135.0 33.6 %collective-permute-start.9 = (bf16[256,1024]{1,0:T(8,128)(2,1)S(1)}, bf16[256,1024]{1,0:T(8,128)(2,1)S(1)}, u32[]{:S(2)}, u32[]{:S(2)}) collective-permute-start(bf16[256,1024]{1,0:T(8,128)(2,1)S(1)} %get-tuple-element.35), channel_id=1, source_target_pairs={{0,1},{1,2},{2,3},{3,0},{4,5},{5,6},{6,7},{7,4},{8,9},{9,10},{10,1... | collective-permute-start | bytes 1572872 | tf_op jit(solution)/shard_map/ppermute | solution.py:44
  171.6 2.4 copy-start.3
  171.7 638.9 %all-gather.15.cloned.1.call-start = ((), (), s32[]{:S(2)}) async-start(), calls=%async_computation.4 | async-start | bytes 18874368 | tf_op jit(solution)/shard_map/all_gather | solution.py:87
  174.0 23.9 %collective-permute-start.15 = (bf16[256,1024]{1,0:T(8,128)(2,1)S(1)}, bf16[256,1024]{1,0:T(8,128)(2,1)S(1)}, u32[]{:S(2)}, u32[]{:S(2)}) collective-permute-start(bf16[256,1024]{1,0:T(8,128)(2,1)S(1)} %get-tuple-element.23), channel_id=1, source_target_pairs={{0,1},{1,2},{2,3},{3,0},{4,5},{5,6},{6,7},{7,4},{8,9},{9,10},{10,1... | collective-permute-start | bytes 1572872 | tf_op jit(solution)/shard_map/ppermute | solution.py:44
  200.5 26.6 %collective-permute-start.16 = (bf16[256,1024]{1,0:T(8,128)(2,1)S(1)}, bf16[256,1024]{1,0:T(8,128)(2,1)S(1)}, u32[]{:S(2)}, u32[]{:S(2)}) collective-permute-start(bf16[256,1024]{1,0:T(8,128)(2,1)S(1)} %get-tuple-element.19), channel_id=1, source_target_pairs={{0,2},{1,3},{2,0},{3,1},{4,6},{5,7},{6,4},{7,5},{8,10},{9,11},{10,... | collective-permute-start | bytes 1572872 | tf_op jit(solution)/shard_map/ppermute | solution.py:44
  201.4 25.8 %collective-permute-start.18 = (bf16[256,1024]{1,0:T(8,128)(2,1)S(1)}, bf16[256,1024]{1,0:T(8,128)(2,1)S(1)}, u32[]{:S(2)}, u32[]{:S(2)}) collective-permute-start(bf16[256,1024]{1,0:T(8,128)(2,1)S(1)} %get-tuple-element.20), channel_id=1, source_target_pairs={{0,1},{1,2},{2,3},{3,0},{4,5},{5,6},{6,7},{7,4},{8,9},{9,10},{10,1... | collective-permute-start | bytes 1572872 | tf_op jit(solution)/shard_map/ppermute | solution.py:44
  232.1 24.4 %collective-permute-start.17 = (bf16[256,1024]{1,0:T(8,128)(2,1)S(1)}, bf16[256,1024]{1,0:T(8,128)(2,1)S(1)}, u32[]{:S(2)}, u32[]{:S(2)}) collective-permute-start(bf16[256,1024]{1,0:T(8,128)(2,1)S(1)} %get-tuple-element.10), channel_id=1, source_target_pairs={{0,3},{1,0},{2,1},{3,2},{4,7},{5,4},{6,5},{7,6},{8,11},{9,8},{10,9... | collective-permute-start | bytes 1572872 | tf_op jit(solution)/shard_map/ppermute | solution.py:44
  242.9 35.2 %collective-permute-start.19 = (bf16[256,1024]{1,0:T(8,128)(2,1)S(1)}, bf16[256,1024]{1,0:T(8,128)(2,1)S(1)}, u32[]{:S(2)}, u32[]{:S(2)}) collective-permute-start(bf16[256,1024]{1,0:T(8,128)(2,1)S(1)} %get-tuple-element.16), channel_id=1, source_target_pairs={{0,2},{1,3},{2,0},{3,1},{4,6},{5,7},{6,4},{7,5},{8,10},{9,11},{10,... | collective-permute-start | bytes 1572872 | tf_op jit(solution)/shard_map/ppermute | solution.py:44
  244.2 34.0 %collective-permute-start.21 = (bf16[256,1024]{1,0:T(8,128)(2,1)S(1)}, bf16[256,1024]{1,0:T(8,128)(2,1)S(1)}, u32[]{:S(2)}, u32[]{:S(2)}) collective-permute-start(bf16[256,1024]{1,0:T(8,128)(2,1)S(1)} %get-tuple-element.11), channel_id=1, source_target_pairs={{0,1},{1,2},{2,3},{3,0},{4,5},{5,6},{6,7},{7,4},{8,9},{9,10},{10,1... | collective-permute-start | bytes 1572872 | tf_op jit(solution)/shard_map/ppermute | solution.py:44
  281.6 1.3 copy-start.5
  283.0 548.9 %all-gather.17.cloned.1.call-start = ((), (), s32[]{:S(2)}) async-start(), calls=%async_computation.5 | async-start | bytes 18874368 | tf_op jit(solution)/shard_map/all_gather | solution.py:87
  283.0 45.5 %collective-permute-start.10 = (bf16[256,1024]{1,0:T(8,128)(2,1)}, bf16[256,1024]{1,0:T(8,128)(2,1)S(1)}, u32[]{:S(2)}, u32[]{:S(2)}) collective-permute-start(bf16[256,1024]{1,0:T(8,128)(2,1)} %get-tuple-element.42), channel_id=1, source_target_pairs={{0,2},{1,3},{2,0},{3,1},{4,6},{5,7},{6,4},{7,5},{8,10},{9,11},{10,... | collective-permute-start | bytes 1572872 | tf_op jit(solution)/shard_map/ppermute | solution.py:44
  293.8 34.8 %collective-permute-start.8 = (bf16[256,1024]{1,0:T(8,128)(2,1)}, bf16[256,1024]{1,0:T(8,128)(2,1)S(1)}, u32[]{:S(2)}, u32[]{:S(2)}) collective-permute-start(bf16[256,1024]{1,0:T(8,128)(2,1)} %get-tuple-element.39), channel_id=1, source_target_pairs={{0,3},{1,0},{2,1},{3,2},{4,7},{5,4},{6,5},{7,6},{8,11},{9,8},{10,9... | collective-permute-start | bytes 1572872 | tf_op jit(solution)/shard_map/ppermute | solution.py:44
  331.3 521.0 %all-gather.19.cloned.1.call-start = ((), (), s32[]{:S(2)}) async-start(), calls=%async_computation.6 | async-start | bytes 18874368 | tf_op jit(solution)/shard_map/all_gather | solution.py:87
  331.3 17.0 %collective-permute-start.20 = (bf16[256,1024]{1,0:T(8,128)(2,1)}, bf16[256,1024]{1,0:T(8,128)(2,1)S(1)}, u32[]{:S(2)}, u32[]{:S(2)}) collective-permute-start(bf16[256,1024]{1,0:T(8,128)(2,1)} %get-tuple-element.15), channel_id=1, source_target_pairs={{0,3},{1,0},{2,1},{3,2},{4,7},{5,4},{6,5},{7,6},{8,11},{9,8},{10,9... | collective-permute-start | bytes 1572872 | tf_op jit(solution)/shard_map/ppermute | solution.py:44
  332.1 37.0 %collective-permute-start.22 = (bf16[256,1024]{1,0:T(8,128)(2,1)}, bf16[256,1024]{1,0:T(8,128)(2,1)S(1)}, u32[]{:S(2)}, u32[]{:S(2)}) collective-permute-start(bf16[256,1024]{1,0:T(8,128)(2,1)} %get-tuple-element.18), channel_id=1, source_target_pairs={{0,2},{1,3},{2,0},{3,1},{4,6},{5,7},{6,4},{7,5},{8,10},{9,11},{10,... | collective-permute-start | bytes 1572872 | tf_op jit(solution)/shard_map/ppermute | solution.py:44
  371.6 18.2 %copy-start.14 = (s32[8,6]{1,0:T(8,128)S(1)}, s32[8,6]{1,0:T(8,128)}, u32[]{:S(2)}) copy-start(s32[8,6]{1,0:T(8,128)} %param.9) | copy-start | bytes 580
  371.6 19.1 %copy-start.15 = (s32[8]{0:T(128)S(1)}, s32[8]{0:T(128)}, u32[]{:S(2)}) copy-start(s32[8]{0:T(128)} %param.10) | copy-start | bytes 100
  371.7 502.8 %all-gather.21.cloned.1.call-start = ((), (), s32[]{:S(2)}) async-start(), calls=%async_computation.7 | async-start | bytes 18874368 | tf_op jit(solution)/shard_map/all_gather | solution.py:87
  371.7 16.1 %collective-permute-start.11 = (bf16[256,1024]{1,0:T(8,128)(2,1)S(1)}, bf16[256,1024]{1,0:T(8,128)(2,1)S(1)}, u32[]{:S(2)}, u32[]{:S(2)}) collective-permute-start(bf16[256,1024]{1,0:T(8,128)(2,1)S(1)} %get-tuple-element.41), channel_id=1, source_target_pairs={{0,3},{1,0},{2,1},{3,2},{4,7},{5,4},{6,5},{7,6},{8,11},{9,8},{10,9... | collective-permute-start | bytes 1572872 | tf_op jit(solution)/shard_map/ppermute | solution.py:44
  402.5 66.3 %all-to-all-start = ((bf16[8,128,2048]{2,1,0:T(8,128)(2,1)}), bf16[8,128,2048]{2,1,0:T(8,128)(2,1)}, u32[]{:S(2)}, u32[]{:S(2)}) async-start(bf16[8,128,2048]{2,1,0:T(8,128)(2,1)} %select_select_fusion), calls=%async_computation | async-start | bytes 8388608 | tf_op jit(solution)/shard_map/all_to_all | solution.py:65
  407.6 487.3 %all-gather.23.cloned.1.call-start = ((), (), s32[]{:S(2)}) async-start(), calls=%async_computation.8 | async-start | bytes 18874368 | tf_op jit(solution)/shard_map/all_gather | solution.py:87
  407.6 15.8 %collective-permute-start.23 = (bf16[256,1024]{1,0:T(8,128)(2,1)S(1)}, bf16[256,1024]{1,0:T(8,128)(2,1)S(1)}, u32[]{:S(2)}, u32[]{:S(2)}) collective-permute-start(bf16[256,1024]{1,0:T(8,128)(2,1)S(1)} %get-tuple-element.17), channel_id=1, source_target_pairs={{0,3},{1,0},{2,1},{3,2},{4,7},{5,4},{6,5},{7,6},{8,11},{9,8},{10,9... | collective-permute-start | bytes 1572872 | tf_op jit(solution)/shard_map/ppermute | solution.py:44
  424.6 1.4 copy-start
  473.5 6.1 copy-start.6
  479.6 6.0 copy-start.1
  479.6 6.0 copy-start.8
  483.0 70.5 %collective-permute-start.24 = (bf16[768,2048]{1,0:T(8,128)(2,1)}, bf16[768,2048]{1,0:T(8,128)(2,1)}, u32[]{:S(2)}, u32[]{:S(2)}) collective-permute-start(bf16[768,2048]{1,0:T(8,128)(2,1)} %get-tuple-element.56), channel_id=1, source_target_pairs={{0,1},{1,2},{2,3},{3,0},{4,5},{5,6},{6,7},{7,4},{8,9},{9,10},{10,1... | collective-permute-start | bytes 9437192 | tf_op jit(solution)/shard_map/ppermute | solution.py:70
  483.5 271.9 %collective-permute-start.25 = (bf16[768,2048]{1,0:T(8,128)(2,1)}, bf16[768,2048]{1,0:T(8,128)(2,1)}, u32[]{:S(2)}, u32[]{:S(2)}) collective-permute-start(bf16[768,2048]{1,0:T(8,128)(2,1)} %get-tuple-element.56), channel_id=1, source_target_pairs={{0,2},{1,3},{2,0},{3,1},{4,6},{5,7},{6,4},{7,5},{8,10},{9,11},{10,... | collective-permute-start | bytes 9437192 | tf_op jit(solution)/shard_map/ppermute | solution.py:70
  485.1 274.3 %collective-permute-start.26 = (bf16[768,2048]{1,0:T(8,128)(2,1)}, bf16[768,2048]{1,0:T(8,128)(2,1)}, u32[]{:S(2)}, u32[]{:S(2)}) collective-permute-start(bf16[768,2048]{1,0:T(8,128)(2,1)} %get-tuple-element.56), channel_id=1, source_target_pairs={{0,3},{1,0},{2,1},{3,2},{4,7},{5,4},{6,5},{7,6},{8,11},{9,8},{10,9... | collective-permute-start | bytes 9437192 | tf_op jit(solution)/shard_map/ppermute | solution.py:70
  485.6 5.9 copy-start.4
  485.6 5.9 copy-start.10
  894.8 21.4 %copy-start.11 = (bf16[768,512]{1,0:T(8,128)(2,1)S(1)}, bf16[768,512]{1,0:T(8,128)(2,1)}, u32[]{:S(2)}) copy-start(bf16[768,512]{1,0:T(8,128)(2,1)} %copy.12) | copy-start | bytes 2359300
  894.8 21.4 %copy-start.12 = (bf16[768,1024]{1,0:T(8,128)(2,1)S(1)}, bf16[768,1024]{1,0:T(8,128)(2,1)}, u32[]{:S(2)}) copy-start(bf16[768,1024]{1,0:T(8,128)(2,1)} %multiply_convert_fusion.1) | copy-start | bytes 4718596
  (4 other events, 4.1 us)
Sparse Core Ops, SparseCore 0:
  39.5 55.3 all-gather.8
  96.8 54.3 all-gather.10
  171.8 101.2 all-gather.12
  283.1 101.1 all-gather.14
  386.0 127.1 all-gather.16
  514.9 89.8 all-gather.18
  606.7 89.8 all-gather.20
  698.5 89.8 all-gather.22
